TPU v7x, 32 devices: a whole 2x2x4 slice. The times are simulated.
32 devices in a mesh: ax: 16 (over z, x, core), rad: 2 (over y).
Axes of the slice: x: 2, y: 2, z: 4, core: 2. Of those that a mesh axis runs over, the one named last changes fastest.
Arguments:
- field: float32 [4, 256, 128, 256], P(None, 'ax', 'rad'), may hold values from -75 to 75
- start_az: float32 [256, 32], replicated, may hold values from -6 to 6
- start_rad: float32 [128, 32], replicated, may hold values from -6 to 6
Outputs:
- core: float32 [4, 256, 1024], P(None, 'ax', 'rad')
- az_factor: float32 [256, 32], replicated
- rad_factor: float32 [128, 32], replicated
All inputs are finite; a program needn't handle non-finite values.
Results may differ from a plain program's by a relative error of at most 0.0003.
Values sent between devices are 32-bit elements; how exact they have to be, the bound alone decides.
A program may use at most 128 MiB of HBM per device.

v0:
```python
import jax
import jax.numpy as jnp
from jax import lax
from jax.sharding import PartitionSpec as P

ITERS = 3


HIGH = lax.Precision.HIGHEST


def orthonormal(block):
    inner = jnp.dot(block.T, block, precision=HIGH, preferred_element_type=jnp.float32)
    lower = jnp.linalg.cholesky(inner)
    return lax.linalg.triangular_solve(lower, block, left_side=False, lower=True, transpose_a=True)


def shards(field, start_az, start_rad):
    snaps, axial, radial, azim = field.shape
    rank = start_az.shape[1]
    flat = field.reshape(-1, azim)
    az_factor = start_az
    partial_gram = jnp.dot(flat.T, flat, precision=HIGH, preferred_element_type=jnp.float32)
    gram_az = lax.psum(partial_gram, ("ax", "rad"))
    for step in range(ITERS):
        az_factor = orthonormal(
            jnp.dot(gram_az, az_factor, precision=HIGH, preferred_element_type=jnp.float32)
        )
    proj = jnp.dot(flat, az_factor, precision=HIGH, preferred_element_type=jnp.float32).reshape(
        snaps, axial, radial, rank
    )
    rad_factor = start_rad
    local = lax.all_to_all(proj, "rad", split_axis=3, concat_axis=2, tiled=True)
    partial_rad = jnp.einsum("sark,saqk->rq", local, local, precision=HIGH)
    gram_rad = lax.psum(partial_rad, ("ax", "rad"))
    for step in range(ITERS):
        rad_factor = orthonormal(
            jnp.dot(gram_rad, rad_factor, precision=HIGH, preferred_element_type=jnp.float32)
        )
    core = jnp.einsum("sark,rj->sakj", local, rad_factor, precision=HIGH).reshape(snaps, axial, -1)
    return (core, az_factor, rad_factor)


def solution(mesh):
    return jax.shard_map(
        shards,
        mesh=mesh,
        in_specs=(P(None, "ax", "rad", None), P(), P()),
        out_specs=(P(None, "ax", "rad"), P(), P()),
        check_vma=False,
    )
```

profile of v0, /device:TPU:0, one launch (start us, length us, event | category | flops | bytes accessed | tf_op | source)
XLA Modules:
  0.0 343.8 jit_solution(6837700258788334705)
XLA Ops:
  7.2 10.9 %convolution_bitcast_fusion.1 = f32[256,256]{1,0:T(8,128)} fusion(f32[4,16,64,256]{3,2,1,0:T(8,128)} %param.8), kind=kOutput, calls=%fused_computation.1 | convolution fusion | flops 3221225472 | bytes 4456448 | tf_op jit(solution)/shard_map/dot_general | solution.py:23
  18.2 0.2 all-reduce.5.cloned.1.call-start
  18.4 127.6 %all-reduce.3.cloned.1.call-done = f32[256,256]{1,0:T(8,128)} async-done(((f32[256,256]{1,0:T(8,128)}), f32[256,256]{1,0:T(8,128)}) %all-reduce.3.cloned.1.call-update) | async-done | bytes 262160 | tf_op jit(solution)/shard_map/psum | solution.py:24
  146.0 1.3 fusion.26
  147.3 0.2 fusion.27
  147.5 0.1 copy.6
  147.5 2.9 cholesky.104
  150.5 0.6 compare_reduce_fusion.5
  151.1 0.7 fusion.2
  151.8 2.4 custom-call.12
  154.2 0.2 convolution_bitcast_fusion.5
  154.5 1.3 fusion.28
  155.8 0.2 fusion.29
  155.9 0.1 copy.7
  156.0 2.9 cholesky.115
  159.0 0.6 compare_reduce_fusion.4
  159.6 0.7 fusion.3
  160.3 2.4 custom-call.13
  162.7 0.2 convolution_bitcast_fusion.4
  163.0 1.3 fusion.30
  164.3 0.2 fusion.31
  164.4 0.1 copy.8
  164.5 2.9 cholesky.126
  167.5 0.6 compare_reduce_fusion.3
  168.1 0.7 fusion.4
  168.8 2.4 custom-call.14
  171.2 0.2 convolution_bitcast_fusion.3
  171.5 6.0 %convolution_bitcast_fusion = f32[4096,32]{0,1:T(8,128)S(1)} fusion(f32[256,32]{0,1:T(8,128)S(1)} %convolution_bitcast_fusion.3, f32[4096,256]{1,0:T(8,128)} %bitcast.130), kind=kOutput, calls=%fused_computation | convolution fusion | flops 402653184 | bytes 4751360 | tf_op jit(solution)/shard_map/dot_general | solution.py:29
  177.5 0.4 reshape.33
  177.9 0.7 reshape.58
  178.6 9.9 %all_to_all.18 = f32[2,1,65536]{2,1,0:T(1,128)S(1)} all-to-all(f32[2,1,65536]{2,1,0:T(1,128)S(1)} %reshape.58), channel_id=1, replica_groups=mesh['ax'=16,'rad'=2] {'rad'}, dimensions={0} | all-to-all | bytes 1048576 | tf_op jit(solution)/shard_map/all_to_all | solution.py:33
  188.5 0.5 broadcast.50
  189.0 2.3 reduce.4
  191.3 0.6 reshape.59
  192.0 0.8 copy.20
  192.8 0.6 all_to_all.16
  193.4 1.6 convolution_bitcast_fusion.2
  195.0 115.7 %all-reduce.5.cloned.1.call-done = f32[128,128]{1,0:T(8,128)} async-done(((f32[128,128]{1,0:T(8,128)}), f32[128,128]{1,0:T(8,128)}) %all-reduce.5.cloned.1.call-update) | async-done | bytes 65552 | tf_op jit(solution)/shard_map/psum | solution.py:35
  310.8 1.0 fusion.32
  311.8 0.2 fusion.33
  312.0 0.1 copy.10
  312.1 2.9 cholesky.137
  315.0 0.6 compare_reduce_fusion.2
  315.7 0.7 fusion.5
  316.3 2.4 custom-call.15
  318.8 0.2 convolution_bitcast_fusion.7
  319.0 1.0 fusion.34
  320.1 0.2 fusion.35
  320.2 0.1 copy.11
  320.3 2.9 cholesky.148
  323.3 0.6 compare_reduce_fusion.1
  323.9 0.7 fusion.6
  324.6 2.4 custom-call.16
  327.0 0.2 convolution_bitcast_fusion.6
  327.3 1.0 fusion.36
  328.3 0.2 fusion.37
  328.5 0.1 copy.12
  328.6 2.9 cholesky.159
  331.5 0.6 compare_reduce_fusion
  332.2 0.7 fusion.7
  332.8 2.4 custom-call.17
  335.3 0.2 fusion.9
  335.5 0.6 fusion
  336.1 0.9 reshape.34
  (23 shorter events, 0.3 us)
Async XLA Ops:
  7.2 138.8 %copy-start = (f32[256,32]{0,1:T(8,128)S(1)}, f32[256,32]{0,1:T(8,128)}, u32[]{:S(2)}) copy-start(f32[256,32]{0,1:T(8,128)} %param.9) | copy-start | bytes 98308
  7.2 138.8 %all-reduce.3.cloned.1.call-start = ((), (), s32[]{:S(2)}) async-start(), calls=%async_computation.1 | async-start | bytes 524288 | tf_op jit(solution)/shard_map/psum | solution.py:24
  18.2 292.6 %all-reduce.5.cloned.1.call-start = ((), (), s32[]{:S(2)}) async-start(), calls=%async_computation.2 | async-start | bytes 131072 | tf_op jit(solution)/shard_map/psum | solution.py:35
  171.5 17.0 %copy-start.1 = (f32[256,32]{0,1:T(8,128)}, f32[256,32]{0,1:T(8,128)S(1)}, u32[]{:S(2)}) copy-start(f32[256,32]{0,1:T(8,128)S(1)} %convolution_bitcast_fusion.3) | copy-start | bytes 98308
  188.5 122.3 %copy-start.3 = (f32[128,32]{0,1:T(8,128)S(1)}, f32[128,32]{0,1:T(8,128)}, u32[]{:S(2)}) copy-start(f32[128,32]{0,1:T(8,128)} %param.10) | copy-start | bytes 49156
  335.5 1.4 copy-start.2
Sparse Core Ops, SparseCore 0:
  18.3 127.6 all-reduce.2
  195.2 115.5 all-reduce.4
where the time goes:
time: 345 us; the launch traced here: 344 us
  waiting for transfers between devices  243 us (70%)
  other arithmetic  42.5 us (12%)
  matrix products  28.5 us (8%)
  between operations  14.3 us (4%)
  blocking collectives  9.89 us (3%)
  local copies, waits for them, and re-layouts  4.95 us (1%)
    psum x1, waiting for transfers between devices, shards(): gram_az = lax.psum(partial_gram, ('ax', 'rad'))  128 us
    psum x1, waiting for transfers between devices, shards(): gram_rad = lax.psum(partial_rad, ('ax', 'rad'))  116 us
    another operation x18, other arithmetic, orthonormal(): lower = jnp.linalg.cholesky(inner)  21.6 us
    another operation x12, other arithmetic, orthonormal(): lax.linalg.triangular_solve(lower, block, left_side=False, lower=True, tr...  18.5 us
    dot_general x1, matrix products, shards(): jnp.dot(flat.T, flat, precision=HIGH, preferred_element_type=jnp.float32)  10.9 us
    all_to_all x1, blocking collectives, shards(): local = lax.all_to_all(proj, 'rad', split_axis=3, concat_axis=2, tiled=True)  9.89 us
  transfers between devices with their start and end apart: 2, of which 2 were waited for; matrix products, arithmetic and copies ran while one was open for 0% of the time, Pallas kernels for 0%

commit v1 on v0

v1 whole, which is shorter than its diff:
```python
import functools

import jax
import jax.numpy as jnp
from jax import lax
from jax.experimental import pallas as pl
from jax.experimental.pallas import tpu as pltpu
from jax.sharding import PartitionSpec as P

ITERS = 3
LANES = 128
PANEL = 8
HIGH = lax.Precision.HIGHEST
MESH = pl.DeviceIdType.MESH
F32 = jnp.float32
BF16 = jnp.bfloat16
VMEM_LIMIT = 48 * 1024 * 1024


def dot(a, b, ca, cb, precision=HIGH):
    return lax.dot_general(
        a, b, (((ca,), (cb,)), ((), ())), precision=precision, preferred_element_type=F32
    )


def dot16(a, b, ca, cb):
    return dot(a, b, ca, cb, lax.Precision.DEFAULT)


def split(value):
    high = value.astype(BF16)
    return high, (value - high.astype(F32)).astype(BF16)


class Groups:
    def __init__(self, n_ax, n_rad, low):
        self.low = min(low, n_ax)
        self.n_rad = n_rad
        self.near = self.low * n_rad
        self.far = n_ax // self.low

    def place(self):
        ax, rad = lax.axis_index("ax"), lax.axis_index("rad")
        return lax.rem(ax, self.low) * self.n_rad + rad, lax.div(ax, self.low)

    def device(self, near, far):
        return (far * self.low + lax.div(near, self.n_rad), lax.rem(near, self.n_rad))

    def rows(self, total):
        return -(-total // (self.near * 8)) * 8

    def greet(self):
        near, far = self.place()
        barrier = pltpu.get_barrier_semaphore()
        for step in range(1, self.near):
            peer = lax.rem(near + step, self.near)
            pl.semaphore_signal(barrier, inc=1, device_id=self.device(peer, far), device_id_type=MESH)
        for step in range(1, self.far):
            peer = lax.rem(far + step, self.far)
            pl.semaphore_signal(barrier, inc=1, device_id=self.device(near, peer), device_id_type=MESH)

    def meet(self):
        pl.semaphore_wait(pltpu.get_barrier_semaphore(), self.near + self.far - 2)

    def scratch(self, rows):
        return [
            pltpu.VMEM((self.near, rows, LANES), F32),
            pltpu.VMEM((self.far, rows, LANES), F32),
            pltpu.SemaphoreType.DMA((2, self.near)),
            pltpu.SemaphoreType.DMA((2, self.far)),
            pltpu.SemaphoreType.DMA((2, self.near)),
        ]

    def all_sum(self, rows, part, out, terms, pieces, sem_a, sem_b, sem_c):
        near, far = self.place()

        def mine(index):
            return pl.ds(pl.multiple_of(index * rows, 8), rows)

        sent = []
        for step in range(1, self.near):
            peer = lax.rem(near + step, self.near)
            sent.append(pltpu.make_async_remote_copy(
                src_ref=part.at[mine(peer)], dst_ref=terms.at[step],
                send_sem=sem_a.at[0, step], recv_sem=sem_a.at[1, step],
                device_id=self.device(peer, far), device_id_type=MESH))
            sent[-1].start()
        total = part[mine(near), :]
        for step in range(1, self.near):
            sent[step - 1].wait_recv()
            total = total + terms[step]
        pieces[far] = total
        for step in range(1, self.far):
            peer = lax.rem(far + step, self.far)
            sent.append(pltpu.make_async_remote_copy(
                src_ref=pieces.at[far], dst_ref=pieces.at[far],
                send_sem=sem_b.at[0, step], recv_sem=sem_b.at[1, step],
                device_id=self.device(near, peer), device_id_type=MESH))
            sent[-1].start()
        for copy in sent[self.near - 1:]:
            copy.wait_recv()
        total = pieces[0]
        for index in range(1, self.far):
            total = total + pieces[index]
        out[mine(near), :] = total
        last = []
        for step in range(1, self.near):
            peer = lax.rem(near + step, self.near)
            last.append(pltpu.make_async_remote_copy(
                src_ref=out.at[mine(near)], dst_ref=out.at[mine(near)],
                send_sem=sem_c.at[0, step], recv_sem=sem_c.at[1, step],
                device_id=self.device(peer, far), device_id_type=MESH))
            last[-1].start()
        for copy in last:
            copy.wait_recv()
        for copy in sent + last:
            copy.wait_send()


def gram_az_kernel(groups, rows, chunk, field, out, part, *scratch):
    groups.greet()
    count, azim = field.shape
    half = azim // 2

    def add(step, totals):
        cells = field[pl.ds(pl.multiple_of(step * chunk, chunk), chunk), :]
        high, low = split(cells)
        return (
            totals[0] + dot16(high, high, 0, 0) + dot16(low, low, 0, 0),
            totals[1] + dot16(high, low, 0, 0),
        )

    zero = jnp.zeros((azim, azim), F32)
    even, mixed = lax.fori_loop(0, count // chunk, add, (zero, zero))
    gram = even + mixed + mixed.T
    part[0:half] = gram[:half, :half]
    part[half:2 * half] = gram[:half, half:]
    part[2 * half:3 * half] = gram[half:, half:]
    if part.shape[0] > 3 * half:
        part[3 * half:] = jnp.zeros((part.shape[0] - 3 * half, LANES), F32)
    groups.meet()
    groups.all_sum(rows, part, out, *scratch)


def orthonormal(block):
    rank = block.shape[0]
    inner = dot(block, block, 1, 1)
    index = lax.broadcasted_iota(jnp.int32, (rank, LANES), 0)
    done = []
    for start in range(0, rank, PANEL):
        columns = [
            jnp.broadcast_to(inner[:, start + i:start + i + 1], (rank, LANES)) for i in range(PANEL)
        ]
        for i in range(PANEL):
            k = start + i
            pivot = columns[i][k:k + 1, :]
            inv = lax.rsqrt(pivot)
            inv = inv * (1.5 - 0.5 * pivot * inv * inv)
            lower = jnp.where(index > k, columns[i] * inv, 0.0)
            for j in range(i + 1, PANEL):
                columns[j] = columns[j] - lower * lower[start + j:start + j + 1, :]
            wide = jnp.concatenate([inv] * (block.shape[1] // LANES), axis=1)
            row = block[k:k + 1, :] * wide
            done.append(row)
            spread = jnp.concatenate([lower] * (block.shape[1] // LANES), axis=1)
            block = block - spread * row
            inner = inner - lower[:, :rank] * (inner[k:k + 1, :] * inv[:, :rank])
    return jnp.concatenate(done, axis=0)


def iterate(gram, start):
    block = orthonormal(dot(start, gram, 0, 0))
    for _ in range(ITERS - 1):
        block = orthonormal(dot(block, gram, 1, 0))
    return block


def az_kernel(group, field, packed, start, factor, proj):
    cells, radial, azim = field.shape
    rank = start.shape[1]
    half = azim // 2
    width = LANES // radial
    pairs = cells // width
    cross = packed[half:2 * half, :]
    gram = jnp.concatenate([
        jnp.concatenate([packed[0:half, :], cross], axis=1),
        jnp.concatenate([cross.T, packed[2 * half:3 * half, :]], axis=1),
    ], axis=0)
    block = iterate(gram, start[...])
    factor[...] = block.T
    high, low = split(block)
    both = jnp.concatenate([high, low], axis=0)

    def project(step, carry):
        first = step * group
        part = jnp.concatenate(
            [field[pl.ds(e * pairs + first, group)] for e in range(width)], axis=1
        ).reshape(group * LANES, azim)
        f_high, f_low = split(part)
        twice = dot16(both, f_high, 1, 1)
        values = twice[:rank] + twice[rank:] + dot16(high, f_low, 1, 1)
        block = jnp.stack([values[:, i * LANES:(i + 1) * LANES] for i in range(group)], axis=1)
        proj[:, pl.ds(pl.multiple_of(first, 8), group), :] = block
        return carry

    lax.fori_loop(0, pairs // group, project, 0)


def gram_rad_kernel(groups, rows, radial, proj, out, held, part, sems, local_sem, *scratch):
    groups.greet()
    n_rad, local_rank, pairs, _ = proj.shape
    ax, me = lax.axis_index("ax"), lax.axis_index("rad")
    own = pltpu.make_async_copy(proj.at[me], held.at[me], local_sem)
    own.start()
    groups.meet()
    copies = []
    for step in range(1, n_rad):
        peer = lax.rem(me + step, n_rad)
        copies.append(pltpu.make_async_remote_copy(
            src_ref=proj.at[peer], dst_ref=held.at[me],
            send_sem=sems.at[0, step], recv_sem=sems.at[1, step],
            device_id=(ax, peer), device_id_type=MESH))
        copies[-1].start()
    own.wait()
    for copy in copies:
        copy.wait()
    blocks = [held[y].reshape(local_rank * pairs, LANES) for y in range(n_rad)]
    per = LANES // radial
    columns = []
    for y in range(n_rad):
        column = []
        for x in range(n_rad):
            square = dot(blocks[x], blocks[y], 0, 0)
            total = square[:radial, :radial]
            for e in range(1, per):
                total = total + square[e * radial:(e + 1) * radial, e * radial:(e + 1) * radial]
            column.append(total)
        columns.append(jnp.concatenate(column, axis=0))
    size = n_rad * radial
    for c in range(size // LANES):
        part[c * size:(c + 1) * size] = jnp.concatenate(columns[c * per:(c + 1) * per], axis=1)
    groups.all_sum(rows, part, out, *scratch)


def rad_kernel(radial, packed, start, held, factor, core):
    n_rad, local_rank, pairs, _ = held.shape
    size, rank = start.shape
    gram = jnp.concatenate(
        [packed[c * size:(c + 1) * size, :] for c in range(size // LANES)], axis=1
    )
    basis = iterate(gram, start[...]).T
    factor[...] = basis
    per = LANES // radial
    total = None
    for y in range(n_rad):
        own = basis[y * radial:(y + 1) * radial]
        zero = jnp.zeros_like(own)
        spread = jnp.concatenate([
            jnp.concatenate([own if e == f else zero for e in range(per)], axis=0)
            for f in range(per)
        ], axis=1)
        term = dot(held[y].reshape(local_rank * pairs, LANES), spread, 1, 0)
        total = term if total is None else total + term
    for e in range(per):
        core[e * pairs:(e + 1) * pairs, :] = jnp.concatenate([
            total[k * pairs:(k + 1) * pairs, e * rank:(e + 1) * rank] for k in range(local_rank)
        ], axis=1)


def shards(n_ax, n_rad, field, start_az, start_rad):
    snaps, axial, radial, azim = field.shape
    rank = start_az.shape[1]
    cells = snaps * axial
    pairs = cells * radial // LANES
    local_rank = rank // n_rad
    size = n_rad * radial
    groups = Groups(n_ax, n_rad, 4)
    in_vmem = pl.BlockSpec(memory_space=pltpu.VMEM)

    def call(kernel, shapes, scratch, name, collective=None):
        extra = {} if collective is None else dict(collective_id=collective, has_side_effects=True)
        return pl.pallas_call(
            kernel,
            name=name,
            out_shape=[jax.ShapeDtypeStruct(shape, F32) for shape in shapes],
            out_specs=[in_vmem] * len(shapes),
            scratch_shapes=scratch,
            compiler_params=pltpu.CompilerParams(vmem_limit_bytes=VMEM_LIMIT, **extra),
        )

    rows = groups.rows(3 * azim // 2)
    total = groups.near * rows
    (gram_az,) = call(
        functools.partial(gram_az_kernel, groups, rows, 512),
        [(total, LANES)],
        [pltpu.VMEM((total, LANES), F32)] + groups.scratch(rows),
        "gram_az", 0,
    )(field.reshape(-1, azim))
    az_factor, proj = call(
        functools.partial(az_kernel, 8),
        [(azim, rank), (rank, pairs, LANES)], [], "az_factor",
    )(field.reshape(cells, radial, azim), gram_az, start_az)
    rows = groups.rows(size * size // LANES)
    total = groups.near * rows
    shape = (n_rad, local_rank, pairs, LANES)
    gram_rad, held = call(
        functools.partial(gram_rad_kernel, groups, rows, radial),
        [(total, LANES), shape],
        [pltpu.VMEM((total, LANES), F32), pltpu.SemaphoreType.DMA((2, n_rad)),
         pltpu.SemaphoreType.DMA] + groups.scratch(rows),
        "gram_rad", 1,
    )(proj.reshape(shape))
    rad_factor, core = call(
        functools.partial(rad_kernel, radial),
        [(size, rank), (cells, local_rank * rank)], [], "rad_factor",
    )(gram_rad, start_rad, held)
    return core.reshape(snaps, axial, -1), az_factor, rad_factor


def solution(mesh):
    return jax.shard_map(
        functools.partial(shards, mesh.shape["ax"], mesh.shape["rad"]),
        mesh=mesh,
        in_specs=(P(None, "ax", "rad", None), P(), P()),
        out_specs=(P(None, "ax", "rad"), P(), P()),
        check_vma=False,
    )
```

time: 345 us -> 57.2 us (0.17)
  waiting for transfers between devices: 243 us -> 0 us
  Pallas kernels: 0 us -> 51 us
  other arithmetic: 42.5 us -> 0 us
  matrix products: 28.5 us -> 0 us
  between operations: 14.3 us -> 0.66 us
  blocking collectives: 9.89 us -> 0 us
    psum x2 -> x0, waiting for transfers between devices: 243 us -> none  [the longest x1 128 us: shards(): gram_az = lax.psum(partial_gram, ('ax', 'rad'))]
    pallas_call x0 -> x4, Pallas kernels: none -> 51 us  [the longest x1 21.1 us: shards(): call(functools.partial(gram_rad_kernel, groups, rows, radial), [(total, L...]
    another operation x30 -> x0, other arithmetic: 40.1 us -> none  [the longest x18 21.6 us: orthonormal(): lower = jnp.linalg.cholesky(inner)]
    dot_general x16 -> x0, matrix products: 27.1 us -> none  [the longest x1 10.9 us: shards(): jnp.dot(flat.T, flat, precision=HIGH, preferred_element_type=jnp.float32)]
    all_to_all x1 -> x0, blocking collectives: 9.89 us -> none  [shards(): local = lax.all_to_all(proj, 'rad', split_axis=3, concat_axis=2, tiled=True)]
    unnamed x10 -> x6, local copies, waits for them, and re-layouts: 1.34 us -> 5.23 us
  transfers between devices with their start and end apart: 2 -> 0, of which waited for: 2 -> 0; matrix products, arithmetic and copies ran while one was open for 0% -> 0% of each run, Pallas kernels for 0% -> 0%
where the time goes in v1:
time: 57.2 us; the launch traced here: 56.9 us
  Pallas kernels  51 us (89%)
  local copies, waits for them, and re-layouts  5.23 us (9%)
  between operations  0.66 us (1%)
    pallas_call x1, Pallas kernels, shards(): call(functools.partial(gram_rad_kernel, groups, rows, radial), [(total, L...  21.1 us
    pallas_call x1, Pallas kernels, shards(): call(functools.partial(gram_az_kernel, groups, rows, 512), [(total, LANES...  19.1 us
    pallas_call x1, Pallas kernels, shards(): call(functools.partial(az_kernel, 8), [(azim, rank), (rank, pairs, LANES)...  5.75 us
    unnamed x6, local copies, waits for them, and re-layouts  5.23 us
    pallas_call x1, Pallas kernels, shards(): call(functools.partial(rad_kernel, radial), [(size, rank), (cells, local_...  5 us

profile of v1, /device:TPU:0, one launch (start us, length us, event | category | flops | bytes accessed | tf_op | source)
XLA Modules:
  0.0 56.9 jit_solution(3724412497477960052)
XLA Ops:
  0.6 0.8 %copy.7.start = f32[128,32]{1,0:T(8,128)S(1)} copy(f32[128,32]{0,1:T(8,128)} %param.5) | data formatting | bytes 32768 | tf_op args[2]
  1.4 0.9 %copy.6.start = f32[256,32]{1,0:T(8,128)S(1)} copy(f32[256,32]{0,1:T(8,128)} %param.4) | data formatting | bytes 65536 | tf_op args[1]
  2.3 0.0 copy-start
  2.3 2.2 %copy-done = f32[4,16,64,256]{3,2,1,0:T(8,128)S(1)} copy-done((f32[4,16,64,256]{3,2,1,0:T(8,128)S(1)}, f32[4,16,64,256]{3,2,1,0:T(8,128)}, u32[]{:S(2)}) %copy-start) | copy-done | bytes 4194328
  4.5 19.1 %gram_az.1.packed = f32[384,128]{1,0:T(8,128)S(1)} custom-call(f32[4096,256]{1,0:T(8,128)S(1)} %bitcast.4), custom_call_target="tpu_custom_call" | custom-call | tf_op jit(solution)/shard_map/gram_az/pallas_call | solution.py:293
  23.6 5.8 %az_factor.1 = (f32[256,32]{1,0:T(8,128)S(1)}, f32[32,32,128]{2,1,0:T(8,128)S(1)}) custom-call(f32[64,64,256]{2,1,0:T(8,128)S(1)} %bitcast.5, f32[384,128]{1,0:T(8,128)S(1)} %gram_az.1.packed, f32[256,32]{1,0:T(8,128)S(1)} %copy.6.start), custom_call_target="tpu_custom_call" | custom-call | tf_op jit(solution)/shard_map/az_factor/pallas_call | solution.py:299
  29.4 0.7 %copy.8 = f32[256,32]{0,1:T(8,128)} copy(f32[256,32]{1,0:T(8,128)S(1)} %get-tuple-element.16) | data formatting | bytes 65536
  30.1 21.1 %gram_rad.1 = (f32[128,128]{1,0:T(8,128)S(1)}, f32[2,16,32,128]{3,2,1,0:T(8,128)S(1)}) custom-call(f32[2,16,32,128]{3,2,1,0:T(8,128)S(1)} %bitcast.6), custom_call_target="tpu_custom_call" | custom-call | tf_op jit(solution)/shard_map/gram_rad/pallas_call | solution.py:306
  51.2 5.0 %rad_factor.1 = (f32[128,32]{1,0:T(8,128)S(1)}, f32[64,512]{1,0:T(8,128)}) custom-call(f32[128,128]{1,0:T(8,128)S(1)} %get-tuple-element.10.packed, f32[128,32]{1,0:T(8,128)S(1)} %copy.7.start, f32[2,16,32,128]{3,2,1,0:T(8,128)S(1)} %get-tuple-element.11.held), custom_call_target="tpu_custom_call" | custom-call | tf_op jit(solution)/shard_map/rad_factor/pallas_call | solution.py:313
  56.2 0.7 %copy.9 = f32[128,32]{0,1:T(8,128)} copy(f32[128,32]{1,0:T(8,128)S(1)} %get-tuple-element.17) | data formatting | bytes 32768
Async XLA Ops:
  2.3 2.2 %copy-start = (f32[4,16,64,256]{3,2,1,0:T(8,128)S(1)}, f32[4,16,64,256]{3,2,1,0:T(8,128)}, u32[]{:S(2)}) copy-start(f32[4,16,64,256]{3,2,1,0:T(8,128)} %param.3) | copy-start | bytes 12582916

commit v2 on v1

--- a/solution.py
+++ b/solution.py
@@ -10,6 +10,8 @@
 ITERS = 3
 LANES = 128
 PANEL = 8
+CHUNK = 8
+GROUP = 8
 HIGH = lax.Precision.HIGHEST
 MESH = pl.DeviceIdType.MESH
 F32 = jnp.float32
@@ -113,33 +115,7 @@
             last[-1].start()
         for copy in last:
             copy.wait_recv()
-        for copy in sent + last:
-            copy.wait_send()
-
-
-def gram_az_kernel(groups, rows, chunk, field, out, part, *scratch):
-    groups.greet()
-    count, azim = field.shape
-    half = azim // 2
-
-    def add(step, totals):
-        cells = field[pl.ds(pl.multiple_of(step * chunk, chunk), chunk), :]
-        high, low = split(cells)
-        return (
-            totals[0] + dot16(high, high, 0, 0) + dot16(low, low, 0, 0),
-            totals[1] + dot16(high, low, 0, 0),
-        )
-
-    zero = jnp.zeros((azim, azim), F32)
-    even, mixed = lax.fori_loop(0, count // chunk, add, (zero, zero))
-    gram = even + mixed + mixed.T
-    part[0:half] = gram[:half, :half]
-    part[half:2 * half] = gram[:half, half:]
-    part[2 * half:3 * half] = gram[half:, half:]
-    if part.shape[0] > 3 * half:
-        part[3 * half:] = jnp.zeros((part.shape[0] - 3 * half, LANES), F32)
-    groups.meet()
-    groups.all_sum(rows, part, out, *scratch)
+        return sent + last
 
 
 def orthonormal(block):
@@ -168,88 +144,126 @@
     return jnp.concatenate(done, axis=0)
 
 
-def iterate(gram, start):
-    block = orthonormal(dot(start, gram, 0, 0))
-    for _ in range(ITERS - 1):
+def iterate(gram, block):
+    for _ in range(ITERS):
         block = orthonormal(dot(block, gram, 1, 0))
     return block
 
 
-def az_kernel(group, field, packed, start, factor, proj):
+def gram_kernel(groups, rows_az, rows_rad, chunk, group, field, start, factor, out, held,
+                cells_ref, loaded, part_az, packed, proj, part_rad, swap_sems, *scratch):
+    groups.greet()
     cells, radial, azim = field.shape
-    rank = start.shape[1]
+    n_rad, local_rank, pairs, _ = held.shape
+    rank = start.shape[0]
     half = azim // 2
-    width = LANES // radial
-    pairs = cells // width
+    ax, me = lax.axis_index("ax"), lax.axis_index("rad")
+
+    def load(step):
+        where = pl.ds(step * chunk, chunk)
+        return pltpu.make_async_copy(field.at[where], cells_ref.at[where], loaded.at[step])
+
+    for step in range(cells // chunk):
+        load(step).start()
+
+    def add(step, total):
+        load(step).wait()
+        high, low = split(cells_ref[pl.ds(step * chunk, chunk)].reshape(chunk * radial, azim))
+        return total + dot16(high, jnp.concatenate([high, low], axis=1), 0, 0)
+
+    total = lax.fori_loop(0, cells // chunk, add, jnp.zeros((azim, 2 * azim), F32))
+    mixed = total[:, azim:]
+    gram = total[:, :azim] + mixed + mixed.T
+    part_az[0:half] = gram[:half, :half]
+    part_az[half:2 * half] = gram[:half, half:]
+    part_az[2 * half:3 * half] = gram[half:, half:]
+    if part_az.shape[0] > 3 * half:
+        part_az[3 * half:] = jnp.zeros((part_az.shape[0] - 3 * half, LANES), F32)
+    groups.meet()
+    sent = groups.all_sum(rows_az, part_az, packed, *scratch[:5])
+
     cross = packed[half:2 * half, :]
     gram = jnp.concatenate([
         jnp.concatenate([packed[0:half, :], cross], axis=1),
         jnp.concatenate([cross.T, packed[2 * half:3 * half, :]], axis=1),
     ], axis=0)
     block = iterate(gram, start[...])
-    factor[...] = block.T
+    factor[...] = block
+
     high, low = split(block)
     both = jnp.concatenate([high, low], axis=0)
-
-    def project(step, carry):
-        first = step * group
-        part = jnp.concatenate(
-            [field[pl.ds(e * pairs + first, group)] for e in range(width)], axis=1
-        ).reshape(group * LANES, azim)
+    width = LANES // radial
+    swaps = []
+    for index in range(pairs // group):
+        first = index * group
+        here = slice(first, first + group)
+        part = jnp.concatenate([
+            cells_ref[e * pairs + first:e * pairs + first + group] for e in range(width)
+        ], axis=1).reshape(group * LANES, azim)
         f_high, f_low = split(part)
         twice = dot16(both, f_high, 1, 1)
         values = twice[:rank] + twice[rank:] + dot16(high, f_low, 1, 1)
-        block = jnp.stack([values[:, i * LANES:(i + 1) * LANES] for i in range(group)], axis=1)
-        proj[:, pl.ds(pl.multiple_of(first, 8), group), :] = block
-        return carry
-
-    lax.fori_loop(0, pairs // group, project, 0)
-
-
-def gram_rad_kernel(groups, rows, radial, proj, out, held, part, sems, local_sem, *scratch):
-    groups.greet()
-    n_rad, local_rank, pairs, _ = proj.shape
-    ax, me = lax.axis_index("ax"), lax.axis_index("rad")
-    own = pltpu.make_async_copy(proj.at[me], held.at[me], local_sem)
-    own.start()
-    groups.meet()
-    copies = []
-    for step in range(1, n_rad):
-        peer = lax.rem(me + step, n_rad)
-        copies.append(pltpu.make_async_remote_copy(
-            src_ref=proj.at[peer], dst_ref=held.at[me],
-            send_sem=sems.at[0, step], recv_sem=sems.at[1, step],
-            device_id=(ax, peer), device_id_type=MESH))
-        copies[-1].start()
-    own.wait()
-    for copy in copies:
-        copy.wait()
-    blocks = [held[y].reshape(local_rank * pairs, LANES) for y in range(n_rad)]
-    per = LANES // radial
+        values = jnp.stack([values[:, i * LANES:(i + 1) * LANES] for i in range(group)], axis=1)
+        for y in range(n_rad):
+            proj[y, :, here, :] = values[y * local_rank:(y + 1) * local_rank]
+        swaps.append([])
+        for step in range(1, n_rad):
+            peer = lax.rem(me + step, n_rad)
+            copy = pltpu.make_async_remote_copy(
+                src_ref=proj.at[peer, :, pl.ds(first, group), :],
+                dst_ref=held.at[me, :, pl.ds(first, group), :],
+                send_sem=swap_sems.at[0, index, step], recv_sem=swap_sems.at[1, index, step],
+                device_id=(ax, peer), device_id_type=MESH)
+            copy.start()
+            swaps[-1].append(copy)
+    held[me] = proj[me]
+
+    square = None
+    for index in range(pairs // group):
+        here = slice(index * group, (index + 1) * group)
+        for copy in swaps[index]:
+            copy.wait_recv()
+        high, low = split(jnp.concatenate([
+            held[y, :, here, :].reshape(local_rank * group, LANES) for y in range(n_rad)
+        ], axis=1))
+        term = dot16(jnp.concatenate([high, low, high], axis=0),
+                     jnp.concatenate([high, high, low], axis=0), 0, 0)
+        square = term if square is None else square + term
     columns = []
     for y in range(n_rad):
         column = []
         for x in range(n_rad):
-            square = dot(blocks[x], blocks[y], 0, 0)
-            total = square[:radial, :radial]
-            for e in range(1, per):
-                total = total + square[e * radial:(e + 1) * radial, e * radial:(e + 1) * radial]
-            column.append(total)
+            terms = [
+                square[x * LANES + e * radial:x * LANES + (e + 1) * radial,
+                       y * LANES + e * radial:y * LANES + (e + 1) * radial]
+                for e in range(width)
+            ]
+            column.append(functools.reduce(jnp.add, terms))
         columns.append(jnp.concatenate(column, axis=0))
     size = n_rad * radial
     for c in range(size // LANES):
-        part[c * size:(c + 1) * size] = jnp.concatenate(columns[c * per:(c + 1) * per], axis=1)
-    groups.all_sum(rows, part, out, *scratch)
-
-
-def rad_kernel(radial, packed, start, held, factor, core):
+        part_rad[c * size:(c + 1) * size] = jnp.concatenate(
+            columns[c * width:(c + 1) * width], axis=1)
+    used = size * size // LANES
+    if part_rad.shape[0] > used:
+        part_rad[used:] = jnp.zeros((part_rad.shape[0] - used, LANES), F32)
+    sent += groups.all_sum(rows_rad, part_rad, out, *scratch[5:])
+    for copies in swaps:
+        sent += copies
+    for copy in sent:
+        copy.wait_send()
+
+
+def rad_kernel(radial, packed, start, held, az_in, az_factor, factor, core):
     n_rad, local_rank, pairs, _ = held.shape
-    size, rank = start.shape
+    rank, size = start.shape
+    az_factor[...] = az_in[...]
     gram = jnp.concatenate(
         [packed[c * size:(c + 1) * size, :] for c in range(size // LANES)], axis=1
     )
-    basis = iterate(gram, start[...]).T
-    factor[...] = basis
+    block = iterate(gram, start[...])
+    factor[...] = block
+    basis = block.T
     per = LANES // radial
     total = None
     for y in range(n_rad):
@@ -276,45 +290,46 @@
     size = n_rad * radial
     groups = Groups(n_ax, n_rad, 4)
     in_vmem = pl.BlockSpec(memory_space=pltpu.VMEM)
-
-    def call(kernel, shapes, scratch, name, collective=None):
-        extra = {} if collective is None else dict(collective_id=collective, has_side_effects=True)
+    in_hbm = pl.BlockSpec(memory_space=pltpu.HBM)
+
+    def call(kernel, in_specs, shapes, scratch, name, **extra):
         return pl.pallas_call(
             kernel,
             name=name,
+            in_specs=in_specs,
             out_shape=[jax.ShapeDtypeStruct(shape, F32) for shape in shapes],
             out_specs=[in_vmem] * len(shapes),
             scratch_shapes=scratch,
             compiler_params=pltpu.CompilerParams(vmem_limit_bytes=VMEM_LIMIT, **extra),
         )
 
-    rows = groups.rows(3 * azim // 2)
-    total = groups.near * rows
-    (gram_az,) = call(
-        functools.partial(gram_az_kernel, groups, rows, 512),
-        [(total, LANES)],
-        [pltpu.VMEM((total, LANES), F32)] + groups.scratch(rows),
-        "gram_az", 0,
-    )(field.reshape(-1, azim))
-    az_factor, proj = call(
-        functools.partial(az_kernel, 8),
-        [(azim, rank), (rank, pairs, LANES)], [], "az_factor",
-    )(field.reshape(cells, radial, azim), gram_az, start_az)
-    rows = groups.rows(size * size // LANES)
-    total = groups.near * rows
+    rows_az = groups.rows(3 * azim // 2)
+    rows_rad = groups.rows(size * size // LANES)
+    total_az, total_rad = groups.near * rows_az, groups.near * rows_rad
     shape = (n_rad, local_rank, pairs, LANES)
-    gram_rad, held = call(
-        functools.partial(gram_rad_kernel, groups, rows, radial),
-        [(total, LANES), shape],
-        [pltpu.VMEM((total, LANES), F32), pltpu.SemaphoreType.DMA((2, n_rad)),
-         pltpu.SemaphoreType.DMA] + groups.scratch(rows),
-        "gram_rad", 1,
-    )(proj.reshape(shape))
-    rad_factor, core = call(
+    chunk, group = CHUNK, GROUP
+    az_factor, gram_rad, held = call(
+        functools.partial(gram_kernel, groups, rows_az, rows_rad, chunk, group),
+        [in_hbm, in_vmem],
+        [(rank, azim), (total_rad, LANES), shape],
+        [
+            pltpu.VMEM((cells, radial, azim), F32),
+            pltpu.SemaphoreType.DMA((cells // chunk,)),
+            pltpu.VMEM((total_az, LANES), F32),
+            pltpu.VMEM((total_az, LANES), F32),
+            pltpu.VMEM(shape, F32),
+            pltpu.VMEM((total_rad, LANES), F32),
+            pltpu.SemaphoreType.DMA((2, pairs // group, n_rad)),
+        ] + groups.scratch(rows_az) + groups.scratch(rows_rad),
+        "grams", collective_id=0, has_side_effects=True,
+    )(field.reshape(cells, radial, azim), start_az.T)
+    az_factor, rad_factor, core = call(
         functools.partial(rad_kernel, radial),
-        [(size, rank), (cells, local_rank * rank)], [], "rad_factor",
-    )(gram_rad, start_rad, held)
-    return core.reshape(snaps, axial, -1), az_factor, rad_factor
+        [in_vmem] * 4,
+        [(rank, azim), (rank, size), (cells, local_rank * rank)],
+        [], "rad_factor",
+    )(gram_rad, start_rad.T, held, az_factor)
+    return core.reshape(snaps, axial, -1), az_factor.T, rad_factor.T
 
 
 def solution(mesh):

time: 57.2 us -> 50.2 us (0.88)
  Pallas kernels: 51 us -> 46.4 us
  local copies, waits for them, and re-layouts: 5.23 us -> 2.94 us
    pallas_call x4 -> x2, Pallas kernels: 51 us -> 46.4 us  [the longest x1 41.5 us: shards(): call(functools.partial(gram_kernel, groups, rows_az, rows_rad, chunk, gro...]
    unnamed x6, local copies, waits for them, and re-layouts: 5.23 us -> 2.94 us
where the time goes in v2:
time: 50.2 us; the launch traced here: 50 us
  Pallas kernels  46.4 us (92%)
  local copies, waits for them, and re-layouts  2.94 us (6%)
  between operations  0.66 us (1%)
    pallas_call x1, Pallas kernels, shards(): call(functools.partial(gram_kernel, groups, rows_az, rows_rad, chunk, gro...  41.5 us
    pallas_call x1, Pallas kernels, shards(): call(functools.partial(rad_kernel, radial), [in_vmem] * 4, [(rank, azim),...  4.93 us
    unnamed x6, local copies, waits for them, and re-layouts  2.94 us

profile of v2, /device:TPU:0, one launch (start us, length us, event | category | flops | bytes accessed | tf_op | source)
XLA Modules:
  0.0 50.0 jit_solution(10789977516229066094)
XLA Ops:
  0.6 0.0 copy-start
  0.6 2.2 %copy-done = f32[4,16,64,256]{3,2,1,0:T(8,128)S(1)} copy-done((f32[4,16,64,256]{3,2,1,0:T(8,128)S(1)}, f32[4,16,64,256]{3,2,1,0:T(8,128)}, u32[]{:S(2)}) %copy-start) | copy-done | bytes 4194328
  2.8 0.0 copy-start.1
  2.8 0.8 %copy-done.1 = f32[256,32]{0,1:T(8,128)S(1)} copy-done((f32[256,32]{0,1:T(8,128)S(1)}, f32[256,32]{0,1:T(8,128)}, u32[]{:S(2)}) %copy-start.1) | copy-done | bytes 32792
  3.6 0.0 copy-start.2
  3.6 41.5 %grams.1 = (f32[32,256]{1,0:T(8,128)S(1)}, f32[128,128]{1,0:T(8,128)S(1)}, f32[2,16,32,128]{3,2,1,0:T(8,128)S(1)}) custom-call(f32[64,64,256]{2,1,0:T(8,128)S(1)} %bitcast.6, f32[32,256]{1,0:T(8,128)S(1)} %bitcast.7), custom_call_target="tpu_custom_call" | custom-call | tf_op jit(solution)/shard_map/grams/pallas_call | solution.py:311
  45.1 0.0 copy-done.2
  45.1 4.9 %rad_factor.1 = (f32[32,256]{1,0:T(8,128)}, f32[32,128]{1,0:T(8,128)}, f32[64,512]{1,0:T(8,128)}) custom-call(f32[128,128]{1,0:T(8,128)S(1)} %get-tuple-element.9.packed, f32[32,128]{1,0:T(8,128)S(1)} %bitcast.8, f32[2,16,32,128]{3,2,1,0:T(8,128)S(1)} %get-tuple-element.10.held, f32[32,256]{1,0:T(8,128)S(1)} %get-tuple-element.11.az_in), custom_call_target="tpu_custom_call" | custom-call | tf_op jit(solution)/shard_map/rad_factor/pallas_call | solution.py:326
Async XLA Ops:
  0.6 2.2 %copy-start = (f32[4,16,64,256]{3,2,1,0:T(8,128)S(1)}, f32[4,16,64,256]{3,2,1,0:T(8,128)}, u32[]{:S(2)}) copy-start(f32[4,16,64,256]{3,2,1,0:T(8,128)} %param.3) | copy-start | bytes 12582916
  2.8 0.8 %copy-start.1 = (f32[256,32]{0,1:T(8,128)S(1)}, f32[256,32]{0,1:T(8,128)}, u32[]{:S(2)}) copy-start(f32[256,32]{0,1:T(8,128)} %param.4) | copy-start | bytes 98308
  3.6 41.5 %copy-start.2 = (f32[128,32]{0,1:T(8,128)S(1)}, f32[128,32]{0,1:T(8,128)}, u32[]{:S(2)}) copy-start(f32[128,32]{0,1:T(8,128)} %param.5) | copy-start | bytes 49156

commit v3 on v2

--- a/solution.py
+++ b/solution.py
@@ -9,7 +9,7 @@
 
 ITERS = 3
 LANES = 128
-PANEL = 8
+PANEL = 32
 CHUNK = 8
 GROUP = 8
 HIGH = lax.Precision.HIGHEST
@@ -145,13 +145,17 @@
 
 
 def iterate(gram, block):
+    gram_high, gram_low = split(gram)
+    rank = block.shape[0]
     for _ in range(ITERS):
-        block = orthonormal(dot(block, gram, 1, 0))
+        high, low = split(block)
+        twice = dot16(jnp.concatenate([high, low], axis=0), gram_high, 1, 0)
+        block = orthonormal(twice[:rank] + twice[rank:] + dot16(high, gram_low, 1, 0))
     return block
 
 
 def gram_kernel(groups, rows_az, rows_rad, chunk, group, field, start, factor, out, held,
-                cells_ref, loaded, part_az, packed, proj, part_rad, swap_sems, *scratch):
+                part_az, packed, proj, part_rad, swap_sems, *scratch):
     groups.greet()
     cells, radial, azim = field.shape
     n_rad, local_rank, pairs, _ = held.shape
@@ -159,16 +163,8 @@
     half = azim // 2
     ax, me = lax.axis_index("ax"), lax.axis_index("rad")
 
-    def load(step):
-        where = pl.ds(step * chunk, chunk)
-        return pltpu.make_async_copy(field.at[where], cells_ref.at[where], loaded.at[step])
-
-    for step in range(cells // chunk):
-        load(step).start()
-
     def add(step, total):
-        load(step).wait()
-        high, low = split(cells_ref[pl.ds(step * chunk, chunk)].reshape(chunk * radial, azim))
+        high, low = split(field[pl.ds(step * chunk, chunk)].reshape(chunk * radial, azim))
         return total + dot16(high, jnp.concatenate([high, low], axis=1), 0, 0)
 
     total = lax.fori_loop(0, cells // chunk, add, jnp.zeros((azim, 2 * azim), F32))
@@ -198,7 +194,7 @@
         first = index * group
         here = slice(first, first + group)
         part = jnp.concatenate([
-            cells_ref[e * pairs + first:e * pairs + first + group] for e in range(width)
+            field[e * pairs + first:e * pairs + first + group] for e in range(width)
         ], axis=1).reshape(group * LANES, azim)
         f_high, f_low = split(part)
         twice = dot16(both, f_high, 1, 1)
@@ -290,7 +286,6 @@
     size = n_rad * radial
     groups = Groups(n_ax, n_rad, 4)
     in_vmem = pl.BlockSpec(memory_space=pltpu.VMEM)
-    in_hbm = pl.BlockSpec(memory_space=pltpu.HBM)
 
     def call(kernel, in_specs, shapes, scratch, name, **extra):
         return pl.pallas_call(
@@ -310,11 +305,9 @@
     chunk, group = CHUNK, GROUP
     az_factor, gram_rad, held = call(
         functools.partial(gram_kernel, groups, rows_az, rows_rad, chunk, group),
-        [in_hbm, in_vmem],
+        [in_vmem, in_vmem],
         [(rank, azim), (total_rad, LANES), shape],
         [
-            pltpu.VMEM((cells, radial, azim), F32),
-            pltpu.SemaphoreType.DMA((cells // chunk,)),
             pltpu.VMEM((total_az, LANES), F32),
             pltpu.VMEM((total_az, LANES), F32),
             pltpu.VMEM(shape, F32),

time: 50.2 us -> 48.5 us (0.966)
  Pallas kernels: 46.4 us -> 44.7 us
    pallas_call x1, Pallas kernels: 41.5 us -> 40.3 us  [shards(): call(functools.partial(gram_kernel, groups, rows_az, rows_rad, chunk, gro...]
    pallas_call x1, Pallas kernels: 4.93 us -> 4.39 us  [shards(): call(functools.partial(rad_kernel, radial), [in_vmem] * 4, [(rank, azim),...]
where the time goes in v3:
time: 48.5 us; the launch traced here: 48.3 us
  Pallas kernels  44.7 us (92%)
  local copies, waits for them, and re-layouts  2.94 us (6%)
  between operations  0.66 us (1%)
    pallas_call x1, Pallas kernels, shards(): call(functools.partial(gram_kernel, groups, rows_az, rows_rad, chunk, gro...  40.3 us
    pallas_call x1, Pallas kernels, shards(): call(functools.partial(rad_kernel, radial), [in_vmem] * 4, [(rank, azim),...  4.39 us
    unnamed x6, local copies, waits for them, and re-layouts  2.94 us

profile of v3, /device:TPU:0, one launch (start us, length us, event | category | flops | bytes accessed | tf_op | source)
XLA Modules:
  0.0 48.3 jit_solution(14088144662216182851)
XLA Ops:
  0.6 0.0 copy-start
  0.6 2.2 %copy-done = f32[4,16,64,256]{3,2,1,0:T(8,128)S(1)} copy-done((f32[4,16,64,256]{3,2,1,0:T(8,128)S(1)}, f32[4,16,64,256]{3,2,1,0:T(8,128)}, u32[]{:S(2)}) %copy-start) | copy-done | bytes 4194328
  2.8 0.0 copy-start.1
  2.8 0.8 %copy-done.1 = f32[256,32]{0,1:T(8,128)S(1)} copy-done((f32[256,32]{0,1:T(8,128)S(1)}, f32[256,32]{0,1:T(8,128)}, u32[]{:S(2)}) %copy-start.1) | copy-done | bytes 32792
  3.6 0.0 copy-start.2
  3.6 40.3 %grams.1 = (f32[32,256]{1,0:T(8,128)S(1)}, f32[128,128]{1,0:T(8,128)S(1)}, f32[2,16,32,128]{3,2,1,0:T(8,128)S(1)}) custom-call(f32[64,64,256]{2,1,0:T(8,128)S(1)} %bitcast.6, f32[32,256]{1,0:T(8,128)S(1)} %bitcast.7), custom_call_target="tpu_custom_call" | custom-call | tf_op jit(solution)/shard_map/grams/pallas_call | solution.py:306
  43.9 0.0 copy-done.2
  43.9 4.4 %rad_factor.1 = (f32[32,256]{1,0:T(8,128)}, f32[32,128]{1,0:T(8,128)}, f32[64,512]{1,0:T(8,128)}) custom-call(f32[128,128]{1,0:T(8,128)S(1)} %get-tuple-element.9.packed, f32[32,128]{1,0:T(8,128)S(1)} %bitcast.8, f32[2,16,32,128]{3,2,1,0:T(8,128)S(1)} %get-tuple-element.10.held, f32[32,256]{1,0:T(8,128)S(1)} %get-tuple-element.11.az_in), custom_call_target="tpu_custom_call" | custom-call | tf_op jit(solution)/shard_map/rad_factor/pallas_call | solution.py:319
Async XLA Ops:
  0.6 2.2 %copy-start = (f32[4,16,64,256]{3,2,1,0:T(8,128)S(1)}, f32[4,16,64,256]{3,2,1,0:T(8,128)}, u32[]{:S(2)}) copy-start(f32[4,16,64,256]{3,2,1,0:T(8,128)} %param.3) | copy-start | bytes 12582916
  2.8 0.8 %copy-start.1 = (f32[256,32]{0,1:T(8,128)S(1)}, f32[256,32]{0,1:T(8,128)}, u32[]{:S(2)}) copy-start(f32[256,32]{0,1:T(8,128)} %param.4) | copy-start | bytes 98308
  3.6 40.3 %copy-start.2 = (f32[128,32]{0,1:T(8,128)S(1)}, f32[128,32]{0,1:T(8,128)}, u32[]{:S(2)}) copy-start(f32[128,32]{0,1:T(8,128)} %param.5) | copy-start | bytes 49156

commit v4 on v3

--- a/solution.py
+++ b/solution.py
@@ -10,7 +10,7 @@
 ITERS = 3
 LANES = 128
 PANEL = 32
-CHUNK = 8
+CHUNK = 32
 GROUP = 8
 HIGH = lax.Precision.HIGHEST
 MESH = pl.DeviceIdType.MESH
@@ -32,6 +32,12 @@
 def split(value):
     high = value.astype(BF16)
     return high, (value - high.astype(F32)).astype(BF16)
+
+
+def dot3(a, b):
+    a_high, a_low = split(a)
+    b_high, b_low = split(b)
+    return dot16(jnp.concatenate([a_high, a_low], axis=1), jnp.concatenate([b_high, b_high], axis=0), 1, 0) + dot16(a_high, b_low, 1, 0)
 
 
 class Groups:
@@ -269,7 +275,7 @@
             jnp.concatenate([own if e == f else zero for e in range(per)], axis=0)
             for f in range(per)
         ], axis=1)
-        term = dot(held[y].reshape(local_rank * pairs, LANES), spread, 1, 0)
+        term = dot3(held[y].reshape(local_rank * pairs, LANES), spread)
         total = term if total is None else total + term
     for e in range(per):
         core[e * pairs:(e + 1) * pairs, :] = jnp.concatenate([

time: 48.5 us -> 47.9 us (0.988)
  Pallas kernels: 44.7 us -> 44.1 us
where the time goes in v4:
time: 47.9 us; the launch traced here: 47.7 us
  Pallas kernels  44.1 us (92%)
  local copies, waits for them, and re-layouts  2.94 us (6%)
  between operations  0.66 us (1%)
    pallas_call x1, Pallas kernels, shards(): call(functools.partial(gram_kernel, groups, rows_az, rows_rad, chunk, gro...  40 us
    pallas_call x1, Pallas kernels, shards(): call(functools.partial(rad_kernel, radial), [in_vmem] * 4, [(rank, azim),...  4.14 us
    unnamed x6, local copies, waits for them, and re-layouts  2.94 us

profile of v4, /device:TPU:0, one launch (start us, length us, event | category | flops | bytes accessed | tf_op | source)
XLA Modules:
  0.0 47.7 jit_solution(1102264242986872526)
XLA Ops:
  0.6 0.0 copy-start
  0.6 2.2 %copy-done = f32[4,16,64,256]{3,2,1,0:T(8,128)S(1)} copy-done((f32[4,16,64,256]{3,2,1,0:T(8,128)S(1)}, f32[4,16,64,256]{3,2,1,0:T(8,128)}, u32[]{:S(2)}) %copy-start) | copy-done | bytes 4194328
  2.8 0.0 copy-start.1
  2.8 0.8 %copy-done.1 = f32[256,32]{0,1:T(8,128)S(1)} copy-done((f32[256,32]{0,1:T(8,128)S(1)}, f32[256,32]{0,1:T(8,128)}, u32[]{:S(2)}) %copy-start.1) | copy-done | bytes 32792
  3.6 0.0 copy-start.2
  3.6 40.0 %grams.1 = (f32[32,256]{1,0:T(8,128)S(1)}, f32[128,128]{1,0:T(8,128)S(1)}, f32[2,16,32,128]{3,2,1,0:T(8,128)S(1)}) custom-call(f32[64,64,256]{2,1,0:T(8,128)S(1)} %bitcast.6, f32[32,256]{1,0:T(8,128)S(1)} %bitcast.7), custom_call_target="tpu_custom_call" | custom-call | tf_op jit(solution)/shard_map/grams/pallas_call | solution.py:312
  43.6 0.0 copy-done.2
  43.6 4.1 %rad_factor.1 = (f32[32,256]{1,0:T(8,128)}, f32[32,128]{1,0:T(8,128)}, f32[64,512]{1,0:T(8,128)}) custom-call(f32[128,128]{1,0:T(8,128)S(1)} %get-tuple-element.9.packed, f32[32,128]{1,0:T(8,128)S(1)} %bitcast.8, f32[2,16,32,128]{3,2,1,0:T(8,128)S(1)} %get-tuple-element.10.held, f32[32,256]{1,0:T(8,128)S(1)} %get-tuple-element.11.az_in), custom_call_target="tpu_custom_call" | custom-call | tf_op jit(solution)/shard_map/rad_factor/pallas_call | solution.py:325
Async XLA Ops:
  0.6 2.2 %copy-start = (f32[4,16,64,256]{3,2,1,0:T(8,128)S(1)}, f32[4,16,64,256]{3,2,1,0:T(8,128)}, u32[]{:S(2)}) copy-start(f32[4,16,64,256]{3,2,1,0:T(8,128)} %param.3) | copy-start | bytes 12582916
  2.8 0.8 %copy-start.1 = (f32[256,32]{0,1:T(8,128)S(1)}, f32[256,32]{0,1:T(8,128)}, u32[]{:S(2)}) copy-start(f32[256,32]{0,1:T(8,128)} %param.4) | copy-start | bytes 98308
  3.6 40.0 %copy-start.2 = (f32[128,32]{0,1:T(8,128)S(1)}, f32[128,32]{0,1:T(8,128)}, u32[]{:S(2)}) copy-start(f32[128,32]{0,1:T(8,128)} %param.5) | copy-start | bytes 49156
